TPU v7x, 256 devices: a whole 4x4x8 slice. The times are simulated.
256 devices in a mesh: seq: 16 (over z, x_lo), wt: 16 (over x_hi, y, core).
Axes of the slice: x: 4 (x_hi: 2, x_lo: 2; x = x_hi * 2 + x_lo), y: 4, z: 8, core: 2. Of those that a mesh axis runs over, the one named last changes fastest.
Arguments:
- frames: bfloat16 [4096, 4096], P('seq'), may hold values from -40 to 40
- attn_norm_gain: float32 [4096], replicated, may hold values from 0.1 to 1.9
- qkv_weight: bfloat16 [3, 4096, 4096], P(None, 'seq', 'wt'), may hold values from -4 to 4
- attn_out_weight: bfloat16 [4096, 4096], P('seq', 'wt'), may hold values from -0.125 to 0.125
- conv_norm_gain: float32 [4096], replicated, may hold values from 0.1 to 1.9
- glu_weight: bfloat16 [2, 4096, 4096], P(None, 'seq', 'wt'), may hold values from -0.09375 to 0.09375
- depth_kernel: float32 [31, 4096], P(None, 'wt'), may hold values from -1 to 1
- norm_scale: float32 [4096], P('wt'), may hold values from 0.5 to 2
- norm_shift: float32 [4096], P('wt'), may hold values from -3 to 3
- conv_out_weight: bfloat16 [4096, 4096], P('seq', 'wt'), may hold values from -0.125 to 0.125
Outputs:
- encoded: bfloat16 [4096, 4096], P('seq', 'wt')
All inputs are finite; a program needn't handle non-finite values.
Results may differ from a plain program's by a relative error of at most 0.014.
Values may be sent and summed in bfloat16 or wider, within the bound.
No kernel may reach another device: no remote copies, remote signals or barrier semaphores. Data moves between devices by JAX's collectives and lax.ppermute only.
A program may use at most 64 MiB of HBM per device.

v0:
```python
import jax
import jax.numpy as jnp
from jax import lax
from jax.sharding import PartitionSpec as P

HEAD_DIM = 128


def padded_2(value, sides, width):
    for axis, dim in sides:
        devices, length = (lax.axis_size(axis), value.shape[dim])
        up = [(i, (i + 1) % devices) for i in range(devices - 1)]
        down = [(j, i) for i, j in up]
        last = lax.slice_in_dim(value, length - width, length, axis=dim)
        first = lax.slice_in_dim(value, 0, width, axis=dim)
        before = lax.ppermute(last, axis, up)
        after = lax.ppermute(first, axis, down)
        value = jnp.concatenate([before, value, after], axis=dim)
    return value


def norm_rows(values, gain_vec):
    wide = values.astype(jnp.float32)
    row_mean = jnp.mean(wide, axis=-1, keepdims=True)
    centered = wide - row_mean
    row_var = jnp.mean(centered * centered, axis=-1, keepdims=True)
    return (centered * lax.rsqrt(row_var + 1e-05) * gain_vec).astype(jnp.bfloat16)


def project_in(normed, stacked):
    return jnp.einsum(
        "rd,mdc->rmc",
        normed,
        lax.all_gather(stacked, "seq", axis=1, tiled=True),
        preferred_element_type=jnp.float32,
    )


def project_out(inputs, weight):
    return lax.dot_general(
        inputs,
        lax.all_gather(weight, "seq", axis=0, tiled=True),
        (((1,), (1,)), ((), ())),
        preferred_element_type=jnp.float32,
    )


def feature_share(partial_sums):
    return lax.psum_scatter(
        partial_sums.astype(jnp.bfloat16), "wt", scatter_dimension=1, tiled=True
    ).astype(jnp.float32)


def local(
    frames,
    attn_norm_gain,
    qkv_weight,
    attn_out_weight,
    conv_norm_gain,
    glu_weight,
    depth_kernel,
    norm_scale,
    norm_shift,
    conv_out_weight,
):
    row_count = frames.shape[0]
    col_count = qkv_weight.shape[2]
    heads_here = col_count // HEAD_DIM
    column_start = lax.axis_index("wt") * col_count
    normed = norm_rows(frames, attn_norm_gain)
    projected = project_in(normed, qkv_weight).astype(jnp.bfloat16)
    query_heads = projected[:, 0].reshape(row_count, heads_here, HEAD_DIM)
    keys = projected[:, 1]
    values = projected[:, 2]
    score_scale = HEAD_DIM ** (-0.5)
    key_segment = lax.all_gather(keys, "seq", axis=0, tiled=True)
    value_segment = lax.all_gather(values, "seq", axis=0, tiled=True)
    row_best = jnp.full((heads_here, row_count), -1e30, jnp.float32)
    key_heads = key_segment.reshape(key_segment.shape[0], heads_here, HEAD_DIM)
    value_heads = value_segment.reshape(value_segment.shape[0], heads_here, HEAD_DIM)
    scores = (
        jnp.einsum("qhd,khd->hqk", query_heads, key_heads, preferred_element_type=jnp.float32)
        * score_scale
    )
    new_best = jnp.maximum(row_best, jnp.max(scores, axis=-1))
    exp_weights = jnp.exp(scores - new_best[..., None])
    running_sum = jnp.sum(exp_weights, axis=-1)
    weighted = jnp.einsum(
        "hqk,khd->hqd",
        exp_weights.astype(jnp.bfloat16),
        value_heads,
        preferred_element_type=jnp.float32,
    )
    row_best, running_sum, weighted = (new_best, running_sum, weighted)
    context = (
        (weighted / running_sum[..., None])
        .transpose(1, 0, 2)
        .reshape(row_count, col_count)
        .astype(jnp.bfloat16)
    )
    attended = project_out(context, attn_out_weight)
    share_cols = feature_share(attended)
    frame_cols = lax.dynamic_slice_in_dim(frames, column_start, col_count, 1)
    residual_cols = (frame_cols.astype(jnp.float32) + share_cols).astype(jnp.bfloat16)
    residual_full = lax.all_gather(residual_cols, "wt", axis=1, tiled=True)
    normed_conv = norm_rows(residual_full, conv_norm_gain)
    glu_pair = project_in(normed_conv, glu_weight)
    gated = (glu_pair[:, 0] * jax.nn.sigmoid(glu_pair[:, 1])).astype(jnp.bfloat16)
    rim_width = (depth_kernel.shape[0] - 1) // 2
    padded = padded_2(gated, (("seq", 0),), rim_width).astype(jnp.float32)
    depth_out = jnp.zeros((row_count, col_count), jnp.float32)
    for tap_index in range(depth_kernel.shape[0]):
        depth_out = depth_out + depth_kernel[tap_index] * padded[tap_index : tap_index + row_count]
    shifted = depth_out * norm_scale + norm_shift
    activated = (shifted * jax.nn.sigmoid(shifted)).astype(jnp.bfloat16)
    conv_cols = feature_share(project_out(activated, conv_out_weight))
    residual_cols = lax.dynamic_slice_in_dim(residual_full, column_start, col_count, 1)
    return (residual_cols.astype(jnp.float32) + conv_cols).astype(jnp.bfloat16)


def solution(mesh):
    in_specs = (
        P("seq", None),
        P(),
        P(None, "seq", "wt"),
        P("seq", "wt"),
        P(),
        P(None, "seq", "wt"),
        P(None, "wt"),
        P("wt"),
        P("wt"),
        P("seq", "wt"),
    )
    out_specs = P("seq", "wt")
    return jax.shard_map(local, mesh=mesh, in_specs=in_specs, out_specs=out_specs, check_vma=False)
```

profile of v0, /device:TPU:32, one launch (start us, length us, event | category | flops | bytes accessed | tf_op | source)
XLA Modules:
  0.0 819.5 jit_solution(16398674720940230616)
XLA Ops:
  6.5 2.1 copy.11
  8.7 2.0 convert_reduce_fusion.1
  11.4 156.5 %all-gather.10.cloned.1.call-done = bf16[3,4096,256]{1,2,0:T(8,128)(2,1)} async-done(((bf16[3,256,256]{1,2,0:T(8,128)(2,1)}), bf16[3,4096,256]{1,2,0:T(8,128)(2,1)}) %all-gather.10.cloned.1.call-update) | async-done | bytes 6291472 | tf_op jit(solution)/shard_map/all_gather | solution.py:34
  167.9 4.7 fusion.28
  174.7 85.2 %all-gather.20.cloned.1.call-done = bf16[4096,1,256]{0,2,1:T(8,128)(2,1)} async-done(((bf16[256,1,256]{0,2,1:T(8,128)(2,1)}), bf16[4096,1,256]{0,2,1:T(8,128)(2,1)}) %all-gather.20.cloned.1.call-update) | async-done | bytes 2097168 | tf_op jit(solution)/shard_map/all_gather | solution.py:76
  260.0 3.0 multiply_reduce_fusion
  263.0 3.2 copy-done
  267.7 77.6 %all-gather.22.cloned.1.call-done = bf16[4096,1,256]{0,2,1:T(8,128)(2,1)} async-done(((bf16[256,1,256]{0,2,1:T(8,128)(2,1)}), bf16[4096,1,256]{0,2,1:T(8,128)(2,1)}) %all-gather.22.cloned.1.call-update) | async-done | bytes 2097168 | tf_op jit(solution)/shard_map/all_gather | solution.py:77
  345.3 5.8 fusion.37
  351.1 69.0 %all-gather.12.cloned.1.call-done = bf16[4096,256]{1,0:T(8,128)(2,1)} async-done(((bf16[256,256]{1,0:T(8,128)(2,1)}), bf16[4096,256]{1,0:T(8,128)(2,1)}) %all-gather.12.cloned.1.call-update) | async-done | bytes 2097168 | tf_op jit(solution)/shard_map/all_gather | solution.py:42
  420.2 3.7 convolution_convert_fusion.1
  423.9 77.6 %reduce-scatter.3.cloned.1.call-done = bf16[256,256]{1,0:T(8,128)(2,1)} async-done(((bf16[256,4096]{1,0:T(8,128)(2,1)}), bf16[256,256]{1,0:T(8,128)(2,1)}) %reduce-scatter.3.cloned.1.call-update) | async-done | bytes 131088 | tf_op jit(solution)/shard_map/reduce_scatter | solution.py:49
  501.5 1.6 add_convert_fusion.1
  504.7 50.7 %all-gather.14.cloned.1.call-done = bf16[256,4096]{1,0:T(8,128)(2,1)} async-done(((bf16[256,256]{1,0:T(8,128)(2,1)}), bf16[256,4096]{1,0:T(8,128)(2,1)}) %all-gather.14.cloned.1.call-update) | async-done | bytes 2097168 | tf_op jit(solution)/shard_map/all_gather | solution.py:105
  555.5 2.1 convert_reduce_fusion
  557.6 2.3 fusion.6
  559.9 94.7 %all-gather.16.cloned.1.call-done = bf16[2,4096,256]{2,1,0:T(8,128)(2,1)} async-done(((bf16[2,256,256]{2,1,0:T(8,128)(2,1)}), bf16[2,4096,256]{2,1,0:T(8,128)(2,1)}) %all-gather.16.cloned.1.call-update) | async-done | bytes 4194320 | tf_op jit(solution)/shard_map/all_gather | solution.py:34
  654.6 3.5 fusion.20
  658.2 3.9 collective-permute-start
  662.0 2.9 collective-permute-start.1
  665.0 2.6 collective-permute-done.1
  667.6 61.0 %all-gather.18.cloned.1.call-done = bf16[4096,256]{1,0:T(8,128)(2,1)} async-done(((bf16[256,256]{1,0:T(8,128)(2,1)}), bf16[4096,256]{1,0:T(8,128)(2,1)}) %all-gather.18.cloned.1.call-update) | async-done | bytes 2097168 | tf_op jit(solution)/shard_map/all_gather | solution.py:42
  728.6 4.6 convolution_convert_fusion
  733.2 78.1 %reduce-scatter.5.cloned.1.call-done = bf16[256,256]{1,0:T(8,128)(2,1)} async-done(((bf16[256,4096]{1,0:T(8,128)(2,1)}), bf16[256,256]{1,0:T(8,128)(2,1)}) %reduce-scatter.5.cloned.1.call-update) | async-done | bytes 131088 | tf_op jit(solution)/shard_map/reduce_scatter | solution.py:49
  (49 shorter events, 7.8 us)
Async XLA Ops:
  6.5 4.1 copy-start.1
  6.5 161.3 %copy-start.4 = (f32[4096]{0:T(1024)S(1)}, f32[4096]{0:T(1024)}, u32[]{:S(2)}) copy-start(f32[4096]{0:T(1024)} %param.11) | copy-start | bytes 49156
  6.5 161.3 %all-gather.10.cloned.1.call-start = ((), (), s32[]{:S(2)}) async-start(), calls=%async_computation.2 | async-start | bytes 6684672 | tf_op jit(solution)/shard_map/all_gather | solution.py:34
  8.6 251.3 %all-gather.20.cloned.1.call-start = ((), (), s32[]{:S(2)}) async-start(), calls=%async_computation.9 | async-start | bytes 2228224 | tf_op jit(solution)/shard_map/all_gather | solution.py:76
  173.4 172.0 %all-gather.22.cloned.1.call-start = ((), (), s32[]{:S(2)}) async-start(), calls=%async_computation.10 | async-start | bytes 2228224 | tf_op jit(solution)/shard_map/all_gather | solution.py:77
  174.1 246.1 %all-gather.12.cloned.1.call-start = ((), (), s32[]{:S(2)}) async-start(), calls=%async_computation.3 | async-start | bytes 2228224 | tf_op jit(solution)/shard_map/all_gather | solution.py:42
  174.7 326.9 %reduce-scatter.3.cloned.1.call-start = ((), (), s32[]{:S(2)}) async-start(), calls=%async_computation.4 | async-start | bytes 2228224 | tf_op jit(solution)/shard_map/reduce_scatter | solution.py:49
  262.9 3.2 copy-start
  351.1 153.6 %copy-start.3 = (f32[31,256]{1,0:T(8,128)S(1)}, f32[31,256]{1,0:T(8,128)}, u32[]{:S(2)}) copy-start(f32[31,256]{1,0:T(8,128)} %param.16) | copy-start | bytes 95236
  423.9 230.7 %copy-start.5 = (f32[4096]{0:T(1024)S(1)}, f32[4096]{0:T(1024)}, u32[]{:S(2)}) copy-start(f32[4096]{0:T(1024)} %param.14) | copy-start | bytes 49156
  423.9 131.6 %all-gather.14.cloned.1.call-start = ((), (), s32[]{:S(2)}) async-start(), calls=%async_computation.5 | async-start | bytes 2228224 | tf_op jit(solution)/shard_map/all_gather | solution.py:105
  503.1 151.4 %all-gather.16.cloned.1.call-start = ((), (), s32[]{:S(2)}) async-start(), calls=%async_computation.6 | async-start | bytes 4456448 | tf_op jit(solution)/shard_map/all_gather | solution.py:34
  503.9 224.7 %all-gather.18.cloned.1.call-start = ((), (), s32[]{:S(2)}) async-start(), calls=%async_computation.7 | async-start | bytes 2228224 | tf_op jit(solution)/shard_map/all_gather | solution.py:42
  504.6 306.7 %reduce-scatter.5.cloned.1.call-start = ((), (), s32[]{:S(2)}) async-start(), calls=%async_computation.8 | async-start | bytes 2228224 | tf_op jit(solution)/shard_map/reduce_scatter | solution.py:49
  555.5 99.1 %copy-start.2 = (bf16[256,4096]{1,0:T(8,128)(2,1)S(1)}, bf16[256,4096]{1,0:T(8,128)(2,1)}, u32[]{:S(2)}) copy-start(bf16[256,4096]{1,0:T(8,128)(2,1)} %all-gather.14.cloned.1.call-done) | copy-start | bytes 6291460
  559.9 168.8 %copy-start.6 = (f32[256]{0:T(256)S(1)}, f32[256]{0:T(256)}, u32[]{:S(2)}) copy-start(f32[256]{0:T(256)} %param.18) | copy-start | bytes 3076
  559.9 168.7 %copy-start.7 = (f32[256]{0:T(256)S(1)}, f32[256]{0:T(256)}, u32[]{:S(2)}) copy-start(f32[256]{0:T(256)} %param.17) | copy-start | bytes 3076
  658.2 6.8 collective-permute-start
  662.0 5.5 collective-permute-start.1
Sparse Core Ops, SparseCore 0:
  9.1 158.7 all-gather.9
  173.5 86.4 all-gather.19
  261.7 83.6 all-gather.21
  347.0 73.1 all-gather.11
  424.2 77.2 reduce-scatter.2
  504.3 51.1 all-gather.13
  557.4 97.1 all-gather.15
  656.5 72.0 all-gather.17
  733.4 77.9 reduce-scatter.4
where the time goes:
time: 820 us; the launch traced here: 819 us
  waiting for transfers between devices  756 us (92%)
  matrix products  25.2 us (3%)
  between operations  13.4 us (2%)
  other arithmetic  11.9 us (1%)
    all_gather x2, waiting for transfers between devices, project_in(): lax.all_gather(stacked, 'seq', axis=1, tiled=True)  251 us
    reduce_scatter x2, waiting for transfers between devices, feature_share(): lax.psum_scatter(partial_sums.astype(jnp.bfloat16), 'wt', scatter_dimensi...  156 us
    all_gather x2, waiting for transfers between devices, project_out(): lax.all_gather(weight, 'seq', axis=0, tiled=True)  130 us
    all_gather x1, waiting for transfers between devices, local(): key_segment = lax.all_gather(keys, 'seq', axis=0, tiled=True)  85.2 us
    all_gather x1, waiting for transfers between devices, local(): value_segment = lax.all_gather(values, 'seq', axis=0, tiled=True)  77.6 us
    all_gather x1, waiting for transfers between devices, local(): residual_full = lax.all_gather(residual_cols, 'wt', axis=1, tiled=True)  50.7 us
  transfers between devices with their start and end apart: 11, of which 10 were waited for; matrix products, arithmetic and copies ran while one was open for 3% of the time, Pallas kernels for 0%

commit v1 on v0

--- a/solution.py
+++ b/solution.py
@@ -73,8 +73,11 @@
     keys = projected[:, 1]
     values = projected[:, 2]
     score_scale = HEAD_DIM ** (-0.5)
-    key_segment = lax.all_gather(keys, "seq", axis=0, tiled=True)
-    value_segment = lax.all_gather(values, "seq", axis=0, tiled=True)
+    key_segment, value_segment = jnp.split(
+        lax.all_gather(jnp.concatenate([keys, values], axis=1), "seq", axis=0, tiled=True),
+        [keys.shape[1]],
+        axis=1,
+    )
     row_best = jnp.full((heads_here, row_count), -1e30, jnp.float32)
     key_heads = key_segment.reshape(key_segment.shape[0], heads_here, HEAD_DIM)
     value_heads = value_segment.reshape(value_segment.shape[0], heads_here, HEAD_DIM)

time: 820 us -> 772 us (0.941)
  waiting for transfers between devices: 756 us -> 713 us
    all_gather x2 -> x1, waiting for transfers between devices: 163 us -> 121 us  [local(): lax.all_gather(jnp.concatenate([keys, values], axis=1), 'seq', axis=0, ti...]
  transfers between devices with their start and end apart: 11 -> 10, of which waited for: 10 -> 9; matrix products, arithmetic and copies ran while one was open for 3% -> 2% of each run, Pallas kernels for 0% -> 0%
where the time goes in v1:
time: 772 us; the launch traced here: 771 us
  waiting for transfers between devices  713 us (92%)
  matrix products  19.7 us (3%)
  between operations  13.7 us (2%)
  other arithmetic  12.7 us (2%)
    all_gather x2, waiting for transfers between devices, project_in(): lax.all_gather(stacked, 'seq', axis=1, tiled=True)  251 us
    reduce_scatter x2, waiting for transfers between devices, feature_share(): lax.psum_scatter(partial_sums.astype(jnp.bfloat16), 'wt', scatter_dimensi...  156 us
    all_gather x2, waiting for transfers between devices, project_out(): lax.all_gather(weight, 'seq', axis=0, tiled=True)  131 us
    all_gather x1, waiting for transfers between devices, local(): lax.all_gather(jnp.concatenate([keys, values], axis=1), 'seq', axis=0, ti...  121 us
    all_gather x1, waiting for transfers between devices, local(): residual_full = lax.all_gather(residual_cols, 'wt', axis=1, tiled=True)  50.9 us
  transfers between devices with their start and end apart: 10, of which 9 were waited for; matrix products, arithmetic and copies ran while one was open for 2% of the time, Pallas kernels for 0%

profile of v1, /device:TPU:32, one launch (start us, length us, event | category | flops | bytes accessed | tf_op | source)
XLA Modules:
  0.0 771.5 jit_solution(17229595017992850027)
XLA Ops:
  6.5 2.1 copy.11
  8.7 2.0 convert_reduce_fusion.1
  11.4 156.5 %all-gather.7.cloned.1.call-done = bf16[3,4096,256]{1,2,0:T(8,128)(2,1)} async-done(((bf16[3,256,256]{1,2,0:T(8,128)(2,1)}), bf16[3,4096,256]{1,2,0:T(8,128)(2,1)}) %all-gather.7.cloned.1.call-update) | async-done | bytes 6291472 | tf_op jit(solution)/shard_map/all_gather | solution.py:34
  167.9 4.7 fusion.28
  174.2 120.9 %all-gather.9.cloned.1.call-done = bf16[4096,512]{0,1:T(8,128)(2,1)} async-done(((bf16[256,512]{0,1:T(8,128)(2,1)}), bf16[4096,512]{0,1:T(8,128)(2,1)}) %all-gather.9.cloned.1.call-update) | async-done | bytes 4194320 | tf_op jit(solution)/shard_map/all_gather | solution.py:77
  295.1 2.7 fusion.113
  299.3 1.5 fusion
  300.8 1.8 fusion.37
  302.6 69.4 %all-gather.11.cloned.1.call-done = bf16[4096,256]{1,0:T(8,128)(2,1)} async-done(((bf16[256,256]{1,0:T(8,128)(2,1)}), bf16[4096,256]{1,0:T(8,128)(2,1)}) %all-gather.11.cloned.1.call-update) | async-done | bytes 2097168 | tf_op jit(solution)/shard_map/all_gather | solution.py:42
  372.0 3.7 convolution_convert_fusion.1
  375.8 77.6 %reduce-scatter.3.cloned.1.call-done = bf16[256,256]{1,0:T(8,128)(2,1)} async-done(((bf16[256,4096]{1,0:T(8,128)(2,1)}), bf16[256,256]{1,0:T(8,128)(2,1)}) %reduce-scatter.3.cloned.1.call-update) | async-done | bytes 131088 | tf_op jit(solution)/shard_map/reduce_scatter | solution.py:49
  453.4 1.6 add_convert_fusion.1
  456.5 50.9 %all-gather.13.cloned.1.call-done = bf16[256,4096]{1,0:T(8,128)(2,1)} async-done(((bf16[256,256]{1,0:T(8,128)(2,1)}), bf16[256,4096]{1,0:T(8,128)(2,1)}) %all-gather.13.cloned.1.call-update) | async-done | bytes 2097168 | tf_op jit(solution)/shard_map/all_gather | solution.py:108
  507.3 2.1 convert_reduce_fusion
  509.4 2.3 fusion.6
  511.7 94.5 %all-gather.15.cloned.1.call-done = bf16[2,4096,256]{2,1,0:T(8,128)(2,1)} async-done(((bf16[2,256,256]{2,1,0:T(8,128)(2,1)}), bf16[2,4096,256]{2,1,0:T(8,128)(2,1)}) %all-gather.15.cloned.1.call-update) | async-done | bytes 4194320 | tf_op jit(solution)/shard_map/all_gather | solution.py:34
  606.3 3.5 fusion.20
  609.9 3.8 collective-permute-start
  613.7 2.9 collective-permute-start.1
  616.7 2.5 collective-permute-done.1
  619.3 61.2 %all-gather.17.cloned.1.call-done = bf16[4096,256]{1,0:T(8,128)(2,1)} async-done(((bf16[256,256]{1,0:T(8,128)(2,1)}), bf16[4096,256]{1,0:T(8,128)(2,1)}) %all-gather.17.cloned.1.call-update) | async-done | bytes 2097168 | tf_op jit(solution)/shard_map/all_gather | solution.py:42
  680.5 4.6 convolution_convert_fusion
  685.1 77.9 %reduce-scatter.5.cloned.1.call-done = bf16[256,256]{1,0:T(8,128)(2,1)} async-done(((bf16[256,4096]{1,0:T(8,128)(2,1)}), bf16[256,256]{1,0:T(8,128)(2,1)}) %reduce-scatter.5.cloned.1.call-update) | async-done | bytes 131088 | tf_op jit(solution)/shard_map/reduce_scatter | solution.py:49
  763.0 1.6 add_convert_fusion
  (46 shorter events, 5.4 us)
Async XLA Ops:
  6.5 4.1 copy-start
  6.5 161.3 %copy-start.3 = (f32[4096]{0:T(1024)S(1)}, f32[4096]{0:T(1024)}, u32[]{:S(2)}) copy-start(f32[4096]{0:T(1024)} %param.11) | copy-start | bytes 49156
  6.5 161.3 %all-gather.7.cloned.1.call-start = ((), (), s32[]{:S(2)}) async-start(), calls=%async_computation.2 | async-start | bytes 6684672 | tf_op jit(solution)/shard_map/all_gather | solution.py:34
  8.6 286.5 %all-gather.9.cloned.1.call-start = ((), (), s32[]{:S(2)}) async-start(), calls=%async_computation.3 | async-start | bytes 4456448 | tf_op jit(solution)/shard_map/all_gather | solution.py:77
  173.4 198.6 %all-gather.11.cloned.1.call-start = ((), (), s32[]{:S(2)}) async-start(), calls=%async_computation.4 | async-start | bytes 2228224 | tf_op jit(solution)/shard_map/all_gather | solution.py:42
  174.1 279.3 %reduce-scatter.3.cloned.1.call-start = ((), (), s32[]{:S(2)}) async-start(), calls=%async_computation.5 | async-start | bytes 2228224 | tf_op jit(solution)/shard_map/reduce_scatter | solution.py:49
  302.6 153.8 %copy-start.2 = (f32[31,256]{1,0:T(8,128)S(1)}, f32[31,256]{1,0:T(8,128)}, u32[]{:S(2)}) copy-start(f32[31,256]{1,0:T(8,128)} %param.16) | copy-start | bytes 95236
  375.7 230.6 %copy-start.4 = (f32[4096]{0:T(1024)S(1)}, f32[4096]{0:T(1024)}, u32[]{:S(2)}) copy-start(f32[4096]{0:T(1024)} %param.14) | copy-start | bytes 49156
  375.7 131.6 %all-gather.13.cloned.1.call-start = ((), (), s32[]{:S(2)}) async-start(), calls=%async_computation.6 | async-start | bytes 2228224 | tf_op jit(solution)/shard_map/all_gather | solution.py:108
  455.0 151.2 %all-gather.15.cloned.1.call-start = ((), (), s32[]{:S(2)}) async-start(), calls=%async_computation.7 | async-start | bytes 4456448 | tf_op jit(solution)/shard_map/all_gather | solution.py:34
  455.6 224.9 %all-gather.17.cloned.1.call-start = ((), (), s32[]{:S(2)}) async-start(), calls=%async_computation.8 | async-start | bytes 2228224 | tf_op jit(solution)/shard_map/all_gather | solution.py:42
  456.4 306.7 %reduce-scatter.5.cloned.1.call-start = ((), (), s32[]{:S(2)}) async-start(), calls=%async_computation.9 | async-start | bytes 2228224 | tf_op jit(solution)/shard_map/reduce_scatter | solution.py:49
  507.3 99.0 %copy-start.1 = (bf16[256,4096]{1,0:T(8,128)(2,1)S(1)}, bf16[256,4096]{1,0:T(8,128)(2,1)}, u32[]{:S(2)}) copy-start(bf16[256,4096]{1,0:T(8,128)(2,1)} %all-gather.13.cloned.1.call-done) | copy-start | bytes 6291460
  511.7 168.8 %copy-start.5 = (f32[256]{0:T(256)S(1)}, f32[256]{0:T(256)}, u32[]{:S(2)}) copy-start(f32[256]{0:T(256)} %param.18) | copy-start | bytes 3076
  511.7 168.8 %copy-start.6 = (f32[256]{0:T(256)S(1)}, f32[256]{0:T(256)}, u32[]{:S(2)}) copy-start(f32[256]{0:T(256)} %param.17) | copy-start | bytes 3076
  609.9 6.8 collective-permute-start
  613.7 5.5 collective-permute-start.1
Sparse Core Ops, SparseCore 0:
  9.1 158.7 all-gather.6
  173.5 121.5 all-gather.8
  296.9 75.0 all-gather.10
  376.1 77.3 reduce-scatter.2
  456.1 51.1 all-gather.12
  509.1 97.1 all-gather.14
  608.2 72.2 all-gather.16
  685.3 77.7 reduce-scatter.4
